TPU v7x, 32 devices: a whole 2x2x4 slice. The times are simulated.
32 devices in a mesh: groups: 2 (over x), seq: 8 (over z, y), head: 2 (over core).
Axes of the slice: x: 2, y: 2, z: 4, core: 2. Of those that a mesh axis runs over, the one named last changes fastest.
Arguments:
- queries: float32 [4096, 2048], P(('groups', 'seq'), 'head'), parts along dimension 0, may hold values from -6 to 6
- keys: float32 [4096, 2048], P(('groups', 'seq'), 'head'), parts along dimension 0, may hold values from -0.01171875 to 0.01171875
- values: float32 [4096, 2048], P(('groups', 'seq'), 'head'), parts along dimension 0, may hold values from -6 to 6
- level_weight: float32 [16, 6, 4096], P('head', None, ('groups', 'seq')), parts along dimension 2, may hold values from 0.1 to 1
- prefix_weight: float32 [16, 8, 4096], P('head', None, ('groups', 'seq')), parts along dimension 2, may hold values from 0.1 to 1
- prefix_state: float32 [16, 2048, 128], P('head', 'groups'), parts along dimension 1, may hold values from -0.5 to 0.5
Outputs:
- attended: float32 [4096, 2048], P(('groups', 'seq'), 'head'), parts along dimension 0
There are 2 independent parts, one for each index of `groups`. A program takes and returns all parts, laid end to end along the dimension named above; each array names one. Nothing has to cross between parts.
All inputs are finite; a program needn't handle non-finite values.
Results may differ from a plain program's by a relative error of at most 0.00005.
Values sent between devices are 32-bit elements; how exact they have to be, the bound alone decides.
A program may use at most 128 MiB of HBM per device.

v0:
```python
import jax
import jax.numpy as jnp
from jax import lax
from jax.sharding import PartitionSpec as P

DH = 128
LEVELS = 6
BUCKETS = 8


def swapped(array, axis, stride):
    return lax.ppermute(array, axis, [(i, i ^ 1 << stride) for i in range(lax.axis_size(axis))])


def shards(queries, keys, values, level_weight, prefix_weight, prefix_state):
    highest_level = lax.Precision.HIGHEST
    tok_rows = queries.shape[0]
    head_count = queries.shape[1] // DH
    query_heads = queries.reshape(tok_rows, head_count, DH)
    key_head_count = keys.reshape(tok_rows, head_count, DH)
    value_heads = values.reshape(tok_rows, head_count, DH)
    query_key_scores = jnp.einsum(
        "thd,shd->hts", query_heads, key_head_count, precision=highest_level
    )
    row_index = lax.broadcasted_iota(jnp.int32, (tok_rows, tok_rows), 0)
    col_index = lax.broadcasted_iota(jnp.int32, (tok_rows, tok_rows), 1)
    causal = col_index <= row_index
    query_key_scores = jnp.where(causal[None], query_key_scores, 0.0) * level_weight[:, 0, :, None]
    local_out = jnp.einsum("hts,she->the", query_key_scores, value_heads, precision=highest_level)
    block_memory_state = jnp.einsum(
        "thd,the->hde", key_head_count, value_heads, precision=highest_level
    )
    position = lax.axis_index("seq")
    running = block_memory_state
    collected = []
    for level_bit in range(LEVELS - 1):
        if 1 << level_bit < lax.axis_size("seq"):
            partner = swapped(running, "seq", level_bit)
            upper_half = jnp.right_shift(position, level_bit) & 1 == 1
            collected.append(jnp.where(upper_half, partner, 0.0))
            running = running + partner
        else:
            collected.append(jnp.zeros_like(block_memory_state))
    per_level_states = jnp.stack(collected)
    scaled = jnp.einsum("thd,hlt->hltd", query_heads, level_weight[:, 1:, :])
    level_out = jnp.einsum("hltd,lhde->the", scaled, per_level_states, precision=highest_level)
    weighted = jnp.einsum("thd,hbt->htbd", query_heads, prefix_weight).reshape(
        head_count, tok_rows, BUCKETS * DH
    )
    prefix_out = jnp.einsum("htr,hre->the", weighted, prefix_state, precision=highest_level)
    combined = local_out + level_out + prefix_out
    return combined.reshape(tok_rows, head_count * DH)


def solution(mesh):
    return jax.shard_map(
        shards,
        mesh=mesh,
        in_specs=(
            P(("groups", "seq"), "head"),
            P(("groups", "seq"), "head"),
            P(("groups", "seq"), "head"),
            P("head", None, ("groups", "seq")),
            P("head", None, ("groups", "seq")),
            P("head", "groups", None),
        ),
        out_specs=P(("groups", "seq"), "head"),
        check_vma=False,
    )
```

profile of v0, /device:TPU:0, one launch (start us, length us, event | category | flops | bytes accessed | tf_op | source)
XLA Modules:
  0.0 82.6 jit_solution(12338821892422495612)
XLA Ops:
  0.0 0.0 copy-start
  0.0 0.0 copy-start.6
  0.0 0.0 copy-start.3
  0.0 1.7 %copy.22 = f32[256,1024]{0,1:T(8,128)S(1)} copy(f32[256,1024]{1,0:T(8,128)} %param.7) | data formatting | bytes 2097152 | tf_op jit(solution)/shard_map/reshape | solution.py:20
  1.7 0.0 copy-done
  1.7 2.0 %fusion.30 = f32[8,128,128]{2,1,0:T(8,128)} fusion(f32[256,8,128]{0,2,1:T(8,128)S(1)} %bitcast.62, f32[256,1024]{1,0:T(8,128)S(1)} %copy-done), kind=kOutput, calls=%fused_computation.22 | convolution fusion | flops 402653184 | bytes 2621440 | tf_op jit(solution)/shard_map/thd,the->hde/dot_general | solution.py:30
  3.7 3.0 %collective-permute-start = (f32[8,128,128]{2,1,0:T(8,128)}, f32[8,128,128]{2,1,0:T(8,128)}, u32[]{:S(2)}, u32[]{:S(2)}) collective-permute-start(f32[8,128,128]{2,1,0:T(8,128)} %fusion.30), channel_id=1, source_target_pairs={{0,2},{2,0},{4,6},{6,4},{8,10},{10,8},{12,14},{14,12},{1,3},{3,1},... | collective-permute-start | bytes 1572872 | tf_op jit(solution)/shard_map/ppermute | solution.py:12
  6.7 0.0 copy-done.6
  6.7 1.3 %copy.15 = f32[8,256,8]{2,1,0:T(8,128)} copy(f32[8,256,8]{1,2,0:T(8,128)S(1)} %bitcast.67) | data formatting | bytes 131072 | tf_op jit(solution)/shard_map/shard_map
  8.0 0.0 copy-start.2
  8.0 0.0 copy-done.3
  8.0 0.2 copy.25
  8.2 0.2 copy.14
  8.4 0.8 copy-done.2
  9.2 0.0 copy-start.7
  9.2 5.1 %broadcast_multiply_fusion = f32[8,256,8,128]{3,2,1,0:T(8,128)} fusion(f32[8,256,128]{2,1,0:T(8,128)S(1)} %copy.14, f32[8,256,8]{2,1,0:T(8,128)S(1)} %copy-done.2), kind=kLoop, calls=%fused_computation.3 | loop fusion | flops 2097152 | bytes 9502720 | tf_op jit(solution)/shard_map/thd,hbt->htbd/dot_general | solution.py:47
  14.3 4.6 %collective-permute-done = f32[8,128,128]{2,1,0:T(8,128)} collective-permute-done((f32[8,128,128]{2,1,0:T(8,128)}, f32[8,128,128]{2,1,0:T(8,128)}, u32[]{:S(2)}, u32[]{:S(2)}) %collective-permute-start) | collective-permute-done | bytes 524320 | tf_op jit(solution)/shard_map/ppermute | solution.py:12
  18.9 2.3 %select_bitcast_fusion.2 = (f32[1,8,128,128]{3,2,1,0:T(8,128)}, f32[8,128,128]{2,1,0:T(8,128)}) fusion(f32[8,128,128]{2,1,0:T(8,128)} %collective-permute-done, pred[]{:T(512)S(6)} %eq.9, f32[8,128,128]{2,1,0:T(8,128)} %fusion.30), kind=kLoop, calls=%fused_computation.34 | loop fusion | flops 262144 | bytes 2097153 | tf_op jit(solution)/shard_map/stack | solution.py:44
  21.2 1.8 %collective-permute-start.1 = (f32[8,128,128]{2,1,0:T(8,128)}, f32[8,128,128]{2,1,0:T(8,128)}, u32[]{:S(2)}, u32[]{:S(2)}) collective-permute-start(f32[8,128,128]{2,1,0:T(8,128)} %get-tuple-element.6), channel_id=1, source_target_pairs={{0,4},{2,6},{4,0},{6,2},{8,12},{10,14},{12,8},{14,10},{1,5},{3,7},... | collective-permute-start | bytes 1572872 | tf_op jit(solution)/shard_map/ppermute | solution.py:12
  23.0 0.0 copy-done.7
  23.0 9.3 %reshape.29 = f32[8,256,1024]{2,1,0:T(8,128)} reshape(f32[8,256,8,128]{3,2,1,0:T(8,128)} %broadcast_multiply_fusion) | data formatting | bytes 16777216 | tf_op jit(solution)/shard_map/reshape | solution.py:47
  32.3 0.1 pad.3.clone
  32.4 3.1 %fusion.32 = f32[8,256,256]{2,1,0:T(8,128)S(1)} fusion(f32[256,8,128]{0,2,1:T(8,128)S(1)} %bitcast.63, f32[256,1024]{1,0:T(8,128)} %param.6), kind=kOutput, calls=%fused_computation.24 | convolution fusion | flops 805306368 | bytes 4194304 | tf_op jit(solution)/shard_map/thd,shd->hts/dot_general | solution.py:22
  35.4 0.0 collective-permute-done.1
  35.4 2.1 %select_bitcast_fusion.1 = (f32[1,8,128,128]{3,2,1,0:T(8,128)S(1)}, f32[8,128,128]{2,1,0:T(8,128)}) fusion(f32[8,128,128]{2,1,0:T(8,128)} %collective-permute-done.1, pred[]{:T(512)S(6)} %eq.10, f32[8,128,128]{2,1,0:T(8,128)} %get-tuple-element.6), kind=kLoop, calls=%fused_computation.33 | loop fusion | flops 262144 | bytes 2097153 | tf_op jit(solution)/shard_map/stack | solution.py:44
  37.6 0.0 copy-start.4
  37.6 2.6 %collective-permute-start.2 = (f32[8,128,128]{2,1,0:T(8,128)}, f32[8,128,128]{2,1,0:T(8,128)}, u32[]{:S(2)}, u32[]{:S(2)}) collective-permute-start(f32[8,128,128]{2,1,0:T(8,128)} %get-tuple-element.8), channel_id=1, source_target_pairs={{0,8},{2,10},{4,12},{6,14},{8,0},{10,2},{12,4},{14,6},{1,9},{3,11}... | collective-permute-start | bytes 1572872 | tf_op jit(solution)/shard_map/ppermute | solution.py:12
  40.2 3.7 %fusion.14 = f32[256,8,128]{0,2,1:T(8,128)} fusion(f32[8,256,256]{2,1,0:T(8,128)S(1)} %fusion.32, f32[8,256]{1,0:T(8,128)S(1)} %slice_bitcast_fusion.1, pred[256,256]{1,0:T(8,128)(4,1)S(1)} %iota_compare_fusion, f32[256,1024]{1,0:T(8,128)S(1)} %copy-done), kind=kOutput, calls=%fused_computation.15 | convolution fusion | flops 806354944 | bytes 4268032 | tf_op jit(solution)/shard_map/hts,she->the/dot_general | solution.py:29
  43.8 0.0 copy-done.4
  43.9 1.0 %copy.10 = f32[1,8,128,128]{2,3,0,1:T(8,128)} copy(f32[1,8,128,128]{3,2,1,0:T(8,128)S(1)} %copy-done.4) | data formatting | bytes 1048576 | tf_op jit(solution)/shard_map/stack | solution.py:44
  44.9 0.0 copy-start.5
  44.9 1.0 %copy.11 = f32[1,8,128,128]{2,3,0,1:T(8,128)} copy(f32[1,8,128,128]{3,2,1,0:T(8,128)S(1)} %get-tuple-element.7) | data formatting | bytes 1048576 | tf_op jit(solution)/shard_map/stack | solution.py:44
  45.9 16.6 %collective-permute-done.2 = f32[8,128,128]{2,1,0:T(8,128)} collective-permute-done((f32[8,128,128]{2,1,0:T(8,128)}, f32[8,128,128]{2,1,0:T(8,128)}, u32[]{:S(2)}, u32[]{:S(2)}) %collective-permute-start.2) | collective-permute-done | bytes 524320 | tf_op jit(solution)/shard_map/ppermute | solution.py:12
  62.6 1.0 %copy.12 = f32[1,8,128,128]{2,3,0,1:T(8,128)} copy(f32[1,8,128,128]{3,2,1,0:T(8,128)S(1)} %select_bitcast_fusion) | data formatting | bytes 1048576 | tf_op jit(solution)/shard_map/stack | solution.py:44
  63.6 0.0 copy-done.5
  63.6 0.0 copy-start.1
  63.6 7.2 %fusion.23 = f32[256,8,128]{0,2,1:T(8,128)S(1)} fusion(f32[256,8,128]{0,2,1:T(8,128)} %fusion.14, f32[8,256,128]{2,1,0:T(8,128)S(1)} %copy.14, f32[8,256,5]{1,2,0:T(8,128)S(1)} %copy.13, f32[1,8,128,128]{2,3,0,1:T(8,128)} %copy.12, f32[1,8,128,128]{2,3,0,1:T(8,128)} %copy.11, f32[1,8,128,128]{2,3,0,1:T(8,128)S(1)} %copy-done.5, f32[5]{0:T(128)S(1)} %pad.3.clone), kind=kOutput, calls=%fused_computation.19 | convolution fusion | flops 2016804864 | bytes 4759572 | tf_op jit(solution)/shard_map/hltd,lhde->the/dot_general | solution.py:46
  70.8 0.0 copy-done.1
  70.8 10.5 %fusion.22 = f32[256,8,128]{0,2,1:T(8,128)S(1)} fusion(f32[256,8,128]{0,2,1:T(8,128)S(1)} %fusion.23, f32[8,256,1024]{2,1,0:T(8,128)} %reshape.29, f32[8,1024,128]{2,1,0:T(8,128)S(1)} %copy-done.1), kind=kOutput, calls=%fused_computation.18 | convolution fusion | flops 3221487616 | bytes 14680064 | tf_op jit(solution)/shard_map/htr,hre->the/dot_general | solution.py:50
  81.3 1.3 %copy.18 = f32[256,1024]{1,0:T(8,128)} copy(f32[256,1024]{0,1:T(8,128)S(1)} %bitcast.64) | data formatting | bytes 2097152 | tf_op jit(solution)/shard_map/reshape | solution.py:52
  (6 shorter events, 0.1 us)
Async XLA Ops:
  0.0 1.7 %copy-start = (f32[256,1024]{1,0:T(8,128)S(1)}, f32[256,1024]{1,0:T(8,128)}, u32[]{:S(2)}) copy-start(f32[256,1024]{1,0:T(8,128)} %param.8) | copy-start | bytes 3145732
  0.0 6.7 %copy-start.6 = (f32[8,8,256]{2,1,0:T(8,128)S(1)}, f32[8,8,256]{2,1,0:T(8,128)}, u32[]{:S(2)}) copy-start(f32[8,8,256]{2,1,0:T(8,128)} %param.10) | copy-start | bytes 196612
  0.0 8.0 %copy-start.3 = (f32[256,1024]{1,0:T(8,128)S(1)}, f32[256,1024]{1,0:T(8,128)}, u32[]{:S(2)}) copy-start(f32[256,1024]{1,0:T(8,128)} %param.6) | copy-start | bytes 3145732
  3.7 15.2 %collective-permute-start = (f32[8,128,128]{2,1,0:T(8,128)}, f32[8,128,128]{2,1,0:T(8,128)}, u32[]{:S(2)}, u32[]{:S(2)}) collective-permute-start(f32[8,128,128]{2,1,0:T(8,128)} %fusion.30), channel_id=1, source_target_pairs={{0,2},{2,0},{4,6},{6,4},{8,10},{10,8},{12,14},{14,12},{1,3},{3,1},... | collective-permute-start | bytes 1572872 | tf_op jit(solution)/shard_map/ppermute | solution.py:12
  8.0 1.2 %copy-start.2 = (f32[8,256,8]{2,1,0:T(8,128)S(1)}, f32[8,256,8]{2,1,0:T(8,128)}, u32[]{:S(2)}) copy-start(f32[8,256,8]{2,1,0:T(8,128)} %copy.15) | copy-start | bytes 196612
  9.2 13.8 %copy-start.7 = (f32[8,6,256]{2,0,1:T(8,128)S(1)}, f32[8,6,256]{2,0,1:T(8,128)}, u32[]{:S(2)}) copy-start(f32[8,6,256]{2,0,1:T(8,128)} %param.9) | copy-start | bytes 147460
  21.2 14.3 %collective-permute-start.1 = (f32[8,128,128]{2,1,0:T(8,128)}, f32[8,128,128]{2,1,0:T(8,128)}, u32[]{:S(2)}, u32[]{:S(2)}) collective-permute-start(f32[8,128,128]{2,1,0:T(8,128)} %get-tuple-element.6), channel_id=1, source_target_pairs={{0,4},{2,6},{4,0},{6,2},{8,12},{10,14},{12,8},{14,10},{1,5},{3,7},... | collective-permute-start | bytes 1572872 | tf_op jit(solution)/shard_map/ppermute | solution.py:12
  37.6 6.3 %copy-start.4 = (f32[1,8,128,128]{3,2,1,0:T(8,128)S(1)}, f32[1,8,128,128]{3,2,1,0:T(8,128)}, u32[]{:S(2)}) copy-start(f32[1,8,128,128]{3,2,1,0:T(8,128)} %get-tuple-element.5) | copy-start | bytes 1572868
  37.6 24.9 %collective-permute-start.2 = (f32[8,128,128]{2,1,0:T(8,128)}, f32[8,128,128]{2,1,0:T(8,128)}, u32[]{:S(2)}, u32[]{:S(2)}) collective-permute-start(f32[8,128,128]{2,1,0:T(8,128)} %get-tuple-element.8), channel_id=1, source_target_pairs={{0,8},{2,10},{4,12},{6,14},{8,0},{10,2},{12,4},{14,6},{1,9},{3,11}... | collective-permute-start | bytes 1572872 | tf_op jit(solution)/shard_map/ppermute | solution.py:12
  44.9 18.7 %copy-start.5 = (f32[1,8,128,128]{2,3,0,1:T(8,128)S(1)}, f32[1,8,128,128]{2,3,0,1:T(8,128)}, u32[]{:S(2)}) copy-start(f32[1,8,128,128]{2,3,0,1:T(8,128)} %copy.10) | copy-start | bytes 1572868
  63.6 7.2 %copy-start.1 = (f32[8,1024,128]{2,1,0:T(8,128)S(1)}, f32[8,1024,128]{2,1,0:T(8,128)}, u32[]{:S(2)}) copy-start(f32[8,1024,128]{2,1,0:T(8,128)} %param.11) | copy-start | bytes 12582916
where the time goes:
time: 83 us; the launch traced here: 82.6 us
  matrix products  26.4 us (32%)
  waiting for transfers between devices  21.3 us (26%)
  local copies, waits for them, and re-layouts  18 us (22%)
  other arithmetic  9.53 us (11%)
  starting transfers between devices  7.36 us (9%)
    ppermute x3, waiting for transfers between devices, swapped(): lax.ppermute(array, axis, [(i, i ^ 1 << stride) for i in range(lax.axis_s...  21.3 us
    dot_general x1, matrix products, shards(): jnp.einsum('htr,hre->the', weighted, prefix_state, precision=highest_level)  10.5 us
    reshape x1, local copies, waits for them, and re-layouts, shards(): jnp.einsum('thd,hbt->htbd', query_heads, prefix_weight)  9.27 us
    ppermute x3, starting transfers between devices, swapped(): lax.ppermute(array, axis, [(i, i ^ 1 << stride) for i in range(lax.axis_s...  7.36 us
    dot_general x1, matrix products, shards(): jnp.einsum('hltd,lhde->the', scaled, per_level_states, precision=highest_...  7.18 us
    dot_general x1, other arithmetic, shards(): jnp.einsum('thd,hbt->htbd', query_heads, prefix_weight)  5.08 us
    another operation x3, other arithmetic, shards(): per_level_states = jnp.stack(collected)  4.42 us
    dot_general x1, matrix products, shards(): jnp.einsum('hts,she->the', query_key_scores, value_heads, precision=highe...  3.69 us
  transfers between devices with their start and end apart: 3, of which 2 were waited for; matrix products, arithmetic and copies ran while one was open for 30% of the time, Pallas kernels for 0%

commit v1 on v0

v1 whole, which is shorter than its diff:
```python
import functools

import jax
import jax.numpy as jnp
from jax import lax
from jax.experimental import pallas as pl
from jax.experimental.pallas import tpu as pltpu
from jax.sharding import PartitionSpec as P

DH = 128
WEIGHTS = 16
F32 = jnp.float32
BF16 = jnp.bfloat16


def halves(x):
    high = x.astype(BF16)
    return high, (x - high.astype(F32)).astype(BF16)


def left(x, axis):
    high, low = halves(x)
    return jnp.concatenate([high, low, high], axis=axis)


def right(x, axis):
    high, low = halves(x)
    return jnp.concatenate([high, high, low], axis=axis)


def dot(a, b, dims):
    return lax.dot_general(a, b, (dims, ((), ())), preferred_element_type=F32)


def kernel(
    n, q_hbm, k_hbm, v_hbm, lw_hbm, pw_hbm, ps_hbm, o_hbm,
    q, k, v, lw, pw, ps, acc, wt, run, got, top,
    in_sem, send_sem, recv_sem, top_send, top_recv, out_sem,
):
    bits = n.bit_length() - 1
    stages = bits - 1
    rows = q.shape[0]
    heads = q.shape[1] // DH
    buckets = pw.shape[1]
    me = lax.axis_index("seq")

    def device(position):
        return {"seq": position}

    def cols(h):
        return pl.ds(pl.multiple_of(h * DH, DH), DH)

    def bit(b):
        return jnp.bitwise_and(jnp.right_shift(me, b), 1) == 1

    partners = [jnp.bitwise_xor(me, 1 << b) for b in range(stages)]
    source = (me >= n // 2 - 2) & (me < n // 2)
    upper = me >= n // 2
    onward = (me >= n // 2 - 2) & (me < n - 2)

    loads = [
        pltpu.make_async_copy(a, b, in_sem.at[i])
        for i, (a, b) in enumerate(
            [(k_hbm, k), (v_hbm, v), (q_hbm, q), (lw_hbm, lw), (pw_hbm, pw), (ps_hbm, ps)]
        )
    ]
    for load in loads:
        load.start()

    barrier = pltpu.get_barrier_semaphore()
    for partner in partners:
        pl.semaphore_signal(barrier, inc=1, device_id=device(partner))

    @pl.when(onward)
    def _():
        pl.semaphore_signal(barrier, inc=1, device_id=device(jnp.minimum(me + 2, n - 1)))

    @pl.when(upper)
    def _():
        pl.semaphore_signal(barrier, inc=1, device_id=device(jnp.maximum(me - 2, 0)))

    pl.semaphore_wait(barrier, stages + onward.astype(jnp.int32) + upper.astype(jnp.int32))

    def stage_copy(b, h):
        return pltpu.make_async_remote_copy(
            src_ref=run.at[b, h], dst_ref=got.at[b, h],
            send_sem=send_sem.at[b, h], recv_sem=recv_sem.at[b, h],
            device_id=device(partners[b]),
        )

    def sends(b):
        return jnp.logical_not(bit(b)) if 0 < b == stages - 1 else None

    def receives(b):
        return bit(b) if 0 < b == stages - 1 else None

    def when(cond, fn):
        if cond is None:
            fn()
        else:
            pl.when(cond)(fn)

    def onward_copy(src, h):
        return pltpu.make_async_remote_copy(
            src_ref=src, dst_ref=top.at[h],
            send_sem=top_send.at[0, h], recv_sem=top_recv.at[h],
            device_id=device(jnp.minimum(me + 2, n - 1)),
        )

    def cross_copy(h):
        return pltpu.make_async_remote_copy(
            src_ref=top.at[h], dst_ref=top.at[h],
            send_sem=top_send.at[1, h], recv_sem=top_recv.at[h],
            device_id=device(partners[0]),
        )

    def owner(h):
        return jnp.bitwise_and(h, 1) == jnp.bitwise_and(me, 1)

    loads[0].wait()
    loads[1].wait()

    def states(h, _):
        kh = left(k[:, cols(h)], 0)
        vh = right(v[:, cols(h)], 0)
        run[0, h] = dot(kh, vh, ((0,), (0,)))
        stage_copy(0, h).start()
        return 0

    lax.fori_loop(0, heads, states, 0)

    for load in loads[2:]:
        load.wait()

    def add_level(h, state, index):
        qh = left(q[:, cols(h)], 1)
        acc[:, cols(h)] += wt[h, :, index : index + 1] * dot(qh, right(state, 0), ((1,), (0,)))

    def own(h):
        lv = jnp.concatenate(
            [pw[h], lw[h], jnp.zeros((WEIGHTS - buckets - lw.shape[1], rows), F32)], axis=0
        )
        weights = lv.T
        wt[h, :, 0:WEIGHTS] = weights
        qh = left(q[:, cols(h)], 1)
        kh = right(k[:, cols(h)], 1)
        scores = dot(qh, kh, ((1,), (1,)))
        row = lax.broadcasted_iota(jnp.int32, (rows, rows), 0)
        col = lax.broadcasted_iota(jnp.int32, (rows, rows), 1)
        scores = jnp.where(col <= row, scores, 0.0)
        total = weights[:, buckets : buckets + 1] * dot(
            left(scores, 1), right(v[:, cols(h)], 0), ((1,), (0,))
        )
        for b in range(0, buckets, 2):
            pair = jnp.concatenate(
                [ps[h, c * DH : (c + 1) * DH, :] for c in (b, b + 1)], axis=1
            )
            both = dot(qh, right(pair, 0), ((1,), (0,)))
            total += weights[:, b : b + 1] * both[:, :DH]
            total += weights[:, b + 1 : b + 2] * both[:, DH:]
        acc[:, cols(h)] = total

    def stage(b, h):
        def arrived():
            stage_copy(b, h).wait_recv()
            if b < stages - 1:
                run[b + 1, h] = run[b, h] + got[b, h]
                when(sends(b + 1), lambda: stage_copy(b + 1, h).start())
            else:
                @pl.when(source & owner(h))
                def _():
                    run[b + 1, h] = run[b, h] + got[b, h]
                    onward_copy(run.at[b + 1, h], h).start()

        when(receives(b), arrived)

        @pl.when(bit(b))
        def _():
            add_level(h, got[b, h], buckets + 1 + b)

    def relay(h):
        @pl.when(upper & owner(h))
        def _():
            cross_copy(h).wait_recv()

            @pl.when(onward)
            def _():
                onward_copy(top.at[h], h).start()

            cross_copy(h).start()

    def out_copy(h):
        return pltpu.make_async_copy(acc.at[:, cols(h)], o_hbm.at[:, cols(h)], out_sem.at[h])

    def finish(h):
        @pl.when(upper)
        def _():
            @pl.when(jnp.logical_not(owner(h)))
            def _():
                cross_copy(h).wait_recv()

            add_level(h, top[h], buckets + stages + 1)

        out_copy(h).start()

    def at(h, fn):
        @pl.when((h >= 0) & (h < heads))
        def _():
            fn(h)

    def step(i, _):
        at(i, own)
        for b in range(stages):
            at(i - b, functools.partial(stage, b))
        at(i - stages, relay)
        at(i - stages - 2, finish)
        return 0

    lax.fori_loop(0, heads + stages + 2, step, 0)

    def drain(h, _):
        for b in range(stages):
            when(sends(b), lambda b=b: stage_copy(b, h).wait_send())

        @pl.when(onward & owner(h))
        def _():
            onward_copy(top.at[h], h).wait_send()

        @pl.when(upper & owner(h))
        def _():
            cross_copy(h).wait_send()

        out_copy(h).wait()
        return 0

    lax.fori_loop(0, heads, drain, 0)


def shards(n, queries, keys, values, level_weight, prefix_weight, prefix_state):
    rows, width = queries.shape
    heads = width // DH
    bits = n.bit_length() - 1
    stages = bits - 1
    args = (queries, keys, values, level_weight, prefix_weight, prefix_state)
    state = (heads, DH, DH)
    return pl.pallas_call(
        functools.partial(kernel, n),
        out_shape=jax.ShapeDtypeStruct((rows, width), F32),
        in_specs=[pl.BlockSpec(memory_space=pl.ANY)] * len(args),
        out_specs=pl.BlockSpec(memory_space=pl.ANY),
        scratch_shapes=[pltpu.VMEM(a.shape, F32) for a in args]
        + [
            pltpu.VMEM((rows, width), F32),
            pltpu.VMEM((heads, rows, 128), F32),
            pltpu.VMEM((stages + 1,) + state, F32),
            pltpu.VMEM((stages,) + state, F32),
            pltpu.VMEM(state, F32),
            pltpu.SemaphoreType.DMA((len(args),)),
            pltpu.SemaphoreType.DMA((stages, heads)),
            pltpu.SemaphoreType.DMA((stages, heads)),
            pltpu.SemaphoreType.DMA((2, heads)),
            pltpu.SemaphoreType.DMA((heads,)),
            pltpu.SemaphoreType.DMA((heads,)),
        ],
        compiler_params=pltpu.CompilerParams(
            collective_id=0, has_side_effects=True, vmem_limit_bytes=40 << 20
        ),
        cost_estimate=pl.CostEstimate(flops=2 << 30, bytes_accessed=8 << 20, transcendentals=0),
    )(*args)


def solution(mesh):
    return jax.shard_map(
        functools.partial(shards, mesh.shape["seq"]),
        mesh=mesh,
        in_specs=(
            P(("groups", "seq"), "head"),
            P(("groups", "seq"), "head"),
            P(("groups", "seq"), "head"),
            P("head", None, ("groups", "seq")),
            P("head", None, ("groups", "seq")),
            P("head", "groups", None),
        ),
        out_specs=P(("groups", "seq"), "head"),
        check_vma=False,
    )
```

time: 83 us -> 40.3 us (0.49)
  the two profiles are of different devices: /device:TPU:0 before, /device:TPU:26 now
where the time goes in v1:
time: 40.3 us; the launch traced here: 40 us
  Pallas kernels  31.5 us (78%)
  local copies, waits for them, and re-layouts  8.48 us (21%)
    pallas_call x1, Pallas kernels, shards(): pl.pallas_call(functools.partial(kernel, n), out_shape=jax.ShapeDtypeStru...  31.5 us
    unnamed x12, local copies, waits for them, and re-layouts  8.48 us

profile of v1, /device:TPU:26, one launch (start us, length us, event | category | flops | bytes accessed | tf_op | source)
XLA Modules:
  0.0 40.0 jit_solution(16347778257884355268)
XLA Ops:
  0.0 0.8 %copy.7.lw_hbm = f32[8,6,256]{2,1,0:T(8,128)S(1)} copy(f32[8,6,256]{2,0,1:T(8,128)} %param.9) | data formatting | bytes 98304 | tf_op args[3]
  0.8 0.0 copy-start
  0.8 2.2 %copy-done = f32[8,1024,128]{2,1,0:T(8,128)S(1)} copy-done((f32[8,1024,128]{2,1,0:T(8,128)S(1)}, f32[8,1024,128]{2,1,0:T(8,128)}, u32[]{:S(2)}) %copy-start) | copy-done | bytes 4194328
  3.0 0.0 copy-start.1
  3.0 1.2 %copy-done.1 = f32[256,1024]{1,0:T(8,128)S(1)} copy-done((f32[256,1024]{1,0:T(8,128)S(1)}, f32[256,1024]{1,0:T(8,128)}, u32[]{:S(2)}) %copy-start.1) | copy-done | bytes 1048600
  4.2 0.0 copy-start.2
  4.2 1.2 %copy-done.2 = f32[256,1024]{1,0:T(8,128)S(1)} copy-done((f32[256,1024]{1,0:T(8,128)S(1)}, f32[256,1024]{1,0:T(8,128)}, u32[]{:S(2)}) %copy-start.2) | copy-done | bytes 1048600
  5.5 0.0 copy-start.3
  5.5 1.2 %copy-done.3 = f32[256,1024]{1,0:T(8,128)S(1)} copy-done((f32[256,1024]{1,0:T(8,128)S(1)}, f32[256,1024]{1,0:T(8,128)}, u32[]{:S(2)}) %copy-start.3) | copy-done | bytes 1048600
  6.7 0.0 copy-start.4
  6.7 0.8 %copy-done.4 = f32[8,8,256]{2,1,0:T(8,128)S(1)} copy-done((f32[8,8,256]{2,1,0:T(8,128)S(1)}, f32[8,8,256]{2,1,0:T(8,128)}, u32[]{:S(2)}) %copy-start.4) | copy-done | bytes 65560
  7.5 31.5 %shard_map.64 = f32[256,1024]{1,0:T(8,128)S(1)} custom-call(f32[256,1024]{1,0:T(8,128)S(1)} %copy-done.1, f32[256,1024]{1,0:T(8,128)S(1)} %copy-done.2, f32[256,1024]{1,0:T(8,128)S(1)} %copy-done.3, f32[8,6,256]{2,1,0:T(8,128)S(1)} %copy.7.lw_hbm, f32[8,8,256]{2,1,0:T(8,128)S(1)} %copy-done.4, f32[8,1024,128]{2,1,0:T(8,128)S(1)} %copy-done), custom_call_target="tpu_custom_call" | custom-call | flops 2147483648 | bytes 8388608 | tf_op jit(solution)/shard_map/pallas_call | solution.py:246
  39.0 1.0 %copy.9 = f32[256,1024]{1,0:T(8,128)} copy(f32[256,1024]{1,0:T(8,128)S(1)} %shard_map.64) | data formatting | bytes 2097152
Async XLA Ops:
  0.8 2.2 %copy-start = (f32[8,1024,128]{2,1,0:T(8,128)S(1)}, f32[8,1024,128]{2,1,0:T(8,128)}, u32[]{:S(2)}) copy-start(f32[8,1024,128]{2,1,0:T(8,128)} %ps_hbm.1) | copy-start | bytes 12582916
  3.0 1.2 %copy-start.1 = (f32[256,1024]{1,0:T(8,128)S(1)}, f32[256,1024]{1,0:T(8,128)}, u32[]{:S(2)}) copy-start(f32[256,1024]{1,0:T(8,128)} %q_hbm.1) | copy-start | bytes 3145732
  4.2 1.2 %copy-start.2 = (f32[256,1024]{1,0:T(8,128)S(1)}, f32[256,1024]{1,0:T(8,128)}, u32[]{:S(2)}) copy-start(f32[256,1024]{1,0:T(8,128)} %k_hbm.1) | copy-start | bytes 3145732
  5.5 1.2 %copy-start.3 = (f32[256,1024]{1,0:T(8,128)S(1)}, f32[256,1024]{1,0:T(8,128)}, u32[]{:S(2)}) copy-start(f32[256,1024]{1,0:T(8,128)} %v_hbm.1) | copy-start | bytes 3145732
  6.7 0.8 %copy-start.4 = (f32[8,8,256]{2,1,0:T(8,128)S(1)}, f32[8,8,256]{2,1,0:T(8,128)}, u32[]{:S(2)}) copy-start(f32[8,8,256]{2,1,0:T(8,128)} %pw_hbm.1) | copy-start | bytes 196612

commit v2 on v1

--- a/solution.py
+++ b/solution.py
@@ -138,7 +138,10 @@
 
     def own(h):
         lv = jnp.concatenate(
-            [pw[h], lw[h], jnp.zeros((WEIGHTS - buckets - lw.shape[1], rows), F32)], axis=0
+            [pw[h]]
+            + [lw[level, pl.ds(h, 1), :] for level in range(lw.shape[0])]
+            + [jnp.zeros((WEIGHTS - buckets - lw.shape[0], rows), F32)],
+            axis=0,
         )
         weights = lv.T
         wt[h, :, 0:WEIGHTS] = weights
@@ -241,7 +244,8 @@
     heads = width // DH
     bits = n.bit_length() - 1
     stages = bits - 1
-    args = (queries, keys, values, level_weight, prefix_weight, prefix_state)
+    by_level = jnp.transpose(level_weight, (1, 0, 2))
+    args = (queries, keys, values, by_level, prefix_weight, prefix_state)
     state = (heads, DH, DH)
     return pl.pallas_call(
         functools.partial(kernel, n),
@@ -263,7 +267,7 @@
             pltpu.SemaphoreType.DMA((heads,)),
         ],
         compiler_params=pltpu.CompilerParams(
-            collective_id=0, has_side_effects=True, vmem_limit_bytes=40 << 20
+            collective_id=0, has_side_effects=True, vmem_limit_bytes=63 << 20
         ),
         cost_estimate=pl.CostEstimate(flops=2 << 30, bytes_accessed=8 << 20, transcendentals=0),
     )(*args)

time: 40.3 us -> 34.2 us (0.85)
  local copies, waits for them, and re-layouts: 8.48 us -> 2.31 us
    unnamed x12 -> x1, local copies, waits for them, and re-layouts: 8.48 us -> 2.31 us
where the time goes in v2:
time: 34.2 us; the launch traced here: 34 us
  Pallas kernels  31.7 us (93%)
  local copies, waits for them, and re-layouts  2.31 us (7%)
    pallas_call x1, Pallas kernels, shards(): pl.pallas_call(functools.partial(kernel, n), out_shape=jax.ShapeDtypeStru...  31.7 us
    unnamed x1, local copies, waits for them, and re-layouts  2.31 us

profile of v2, /device:TPU:26, one launch (start us, length us, event | category | flops | bytes accessed | tf_op | source)
XLA Modules:
  0.0 34.0 jit_solution(13245232182009159607)
XLA Ops:
  0.0 31.7 %shard_map.64 = f32[256,1024]{1,0:T(8,128)} custom-call(f32[256,1024]{1,0:T(8,128)} %q_hbm.1, f32[256,1024]{1,0:T(8,128)} %k_hbm.1, f32[256,1024]{1,0:T(8,128)} %v_hbm.1, f32[6,8,256]{2,1,0:T(8,128)} %bitcast.1, f32[8,8,256]{2,1,0:T(8,128)} %pw_hbm.1, f32[8,1024,128]{2,1,0:T(8,128)} %ps_hbm.1), custom_call_target="tpu_custom_call" | custom-call | flops 2147483648 | bytes 8388608 | tf_op jit(solution)/shard_map/pallas_call | solution.py:250
  31.7 2.3 %copy.8 = f32[256,1024]{1,0:T(8,128)} copy(f32[256,1024]{1,0:T(8,128)} %shard_map.64) | data formatting | bytes 2097152

commit v3 on v2

--- a/solution.py
+++ b/solution.py
@@ -114,13 +114,26 @@
             device_id=device(partners[0]),
         )
 
+    mine = jnp.bitwise_and(me, 1)
+
     def owner(h):
-        return jnp.bitwise_and(h, 1) == jnp.bitwise_and(me, 1)
+        return jnp.bitwise_and(h, 1) == mine
+
+    def ordered(j, first):
+        early = j < heads // 2
+        return jnp.where(early, 2 * j + first, 2 * j - heads + 1 - first)
+
+    def arriving(j):
+        return ordered(j, mine)
+
+    def leaving(j):
+        return ordered(j, 1 - mine)
 
     loads[0].wait()
     loads[1].wait()
 
-    def states(h, _):
+    def states(j, _):
+        h = leaving(j)
         kh = left(k[:, cols(h)], 0)
         vh = right(v[:, cols(h)], 0)
         run[0, h] = dot(kh, vh, ((0,), (0,)))
@@ -136,7 +149,8 @@
         qh = left(q[:, cols(h)], 1)
         acc[:, cols(h)] += wt[h, :, index : index + 1] * dot(qh, right(state, 0), ((1,), (0,)))
 
-    def own(h):
+    def own(j):
+        h = arriving(j)
         lv = jnp.concatenate(
             [pw[h]]
             + [lw[level, pl.ds(h, 1), :] for level in range(lw.shape[0])]
@@ -163,7 +177,9 @@
             total += weights[:, b + 1 : b + 2] * both[:, DH:]
         acc[:, cols(h)] = total
 
-    def stage(b, h):
+    def stage(b, j):
+        h = arriving(j)
+
         def arrived():
             stage_copy(b, h).wait_recv()
             if b < stages - 1:
@@ -181,8 +197,10 @@
         def _():
             add_level(h, got[b, h], buckets + 1 + b)
 
-    def relay(h):
-        @pl.when(upper & owner(h))
+    def relay(j):
+        h = jnp.minimum(2 * j + mine, heads - 1)
+
+        @pl.when(upper & (j < heads // 2))
         def _():
             cross_copy(h).wait_recv()
 
@@ -195,7 +213,9 @@
     def out_copy(h):
         return pltpu.make_async_copy(acc.at[:, cols(h)], o_hbm.at[:, cols(h)], out_sem.at[h])
 
-    def finish(h):
+    def finish(j):
+        h = arriving(j)
+
         @pl.when(upper)
         def _():
             @pl.when(jnp.logical_not(owner(h)))

time: 34.2 us -> 30.2 us (0.88)
  Pallas kernels: 31.7 us -> 27.7 us
    pallas_call x1, Pallas kernels: 31.7 us -> 27.7 us  [shards(): pl.pallas_call(functools.partial(kernel, n), out_shape=jax.ShapeDtypeStru...]
where the time goes in v3:
time: 30.2 us; the launch traced here: 30 us
  Pallas kernels  27.7 us (92%)
  local copies, waits for them, and re-layouts  2.31 us (8%)
    pallas_call x1, Pallas kernels, shards(): pl.pallas_call(functools.partial(kernel, n), out_shape=jax.ShapeDtypeStru...  27.7 us
    unnamed x1, local copies, waits for them, and re-layouts  2.31 us

profile of v3, /device:TPU:26, one launch (start us, length us, event | category | flops | bytes accessed | tf_op | source)
XLA Modules:
  0.0 30.0 jit_solution(515529170304979744)
XLA Ops:
  0.0 27.7 %shard_map.64 = f32[256,1024]{1,0:T(8,128)} custom-call(f32[256,1024]{1,0:T(8,128)} %q_hbm.1, f32[256,1024]{1,0:T(8,128)} %k_hbm.1, f32[256,1024]{1,0:T(8,128)} %v_hbm.1, f32[6,8,256]{2,1,0:T(8,128)} %bitcast.1, f32[8,8,256]{2,1,0:T(8,128)} %pw_hbm.1, f32[8,1024,128]{2,1,0:T(8,128)} %ps_hbm.1), custom_call_target="tpu_custom_call" | custom-call | flops 2147483648 | bytes 8388608 | tf_op jit(solution)/shard_map/pallas_call | solution.py:270
  27.7 2.3 %copy.8 = f32[256,1024]{1,0:T(8,128)} copy(f32[256,1024]{1,0:T(8,128)} %shard_map.64) | data formatting | bytes 2097152

commit v4 on v3

--- a/solution.py
+++ b/solution.py
@@ -33,9 +33,9 @@
 
 
 def kernel(
-    n, q_hbm, k_hbm, v_hbm, lw_hbm, pw_hbm, ps_hbm, o_hbm,
-    q, k, v, lw, pw, ps, acc, wt, run, got, top,
-    in_sem, send_sem, recv_sem, top_send, top_recv, out_sem,
+    n, q_hbm, k_hbm, v_hbm, lw_hbm, pw_hbm, ps_hbm, acc,
+    q, k, v, lw, pw, ps, wt, run, got, top,
+    in_sem, send_sem, recv_sem, top_send, top_recv,
 ):
     bits = n.bit_length() - 1
     stages = bits - 1
@@ -88,10 +88,16 @@
             device_id=device(partners[b]),
         )
 
+    last = me >= n - 2
+
     def sends(b):
+        if b == 0 and stages <= 2:
+            return jnp.logical_not(bit(0) & last)
         return jnp.logical_not(bit(b)) if 0 < b == stages - 1 else None
 
     def receives(b):
+        if b == 0 and stages <= 2:
+            return bit(0) | jnp.logical_not(last)
         return bit(b) if 0 < b == stages - 1 else None
 
     def when(cond, fn):
@@ -137,7 +143,7 @@
         kh = left(k[:, cols(h)], 0)
         vh = right(v[:, cols(h)], 0)
         run[0, h] = dot(kh, vh, ((0,), (0,)))
-        stage_copy(0, h).start()
+        when(sends(0), stage_copy(0, h).start)
         return 0
 
     lax.fori_loop(0, heads, states, 0)
@@ -210,9 +216,6 @@
 
             cross_copy(h).start()
 
-    def out_copy(h):
-        return pltpu.make_async_copy(acc.at[:, cols(h)], o_hbm.at[:, cols(h)], out_sem.at[h])
-
     def finish(j):
         h = arriving(j)
 
@@ -223,8 +226,6 @@
                 cross_copy(h).wait_recv()
 
             add_level(h, top[h], buckets + stages + 1)
-
-        out_copy(h).start()
 
     def at(h, fn):
         @pl.when((h >= 0) & (h < heads))
@@ -253,7 +254,6 @@
         def _():
             cross_copy(h).wait_send()
 
-        out_copy(h).wait()
         return 0
 
     lax.fori_loop(0, heads, drain, 0)
@@ -269,12 +269,11 @@
     state = (heads, DH, DH)
     return pl.pallas_call(
         functools.partial(kernel, n),
-        out_shape=jax.ShapeDtypeStruct((rows, width), F32),
+        out_shape=pltpu.VMEM((rows, width), F32),
         in_specs=[pl.BlockSpec(memory_space=pl.ANY)] * len(args),
-        out_specs=pl.BlockSpec(memory_space=pl.ANY),
+        out_specs=pl.BlockSpec(memory_space=pltpu.VMEM),
         scratch_shapes=[pltpu.VMEM(a.shape, F32) for a in args]
         + [
-            pltpu.VMEM((rows, width), F32),
             pltpu.VMEM((heads, rows, 128), F32),
             pltpu.VMEM((stages + 1,) + state, F32),
             pltpu.VMEM((stages,) + state, F32),
@@ -284,10 +283,9 @@
             pltpu.SemaphoreType.DMA((stages, heads)),
             pltpu.SemaphoreType.DMA((2, heads)),
             pltpu.SemaphoreType.DMA((heads,)),
-            pltpu.SemaphoreType.DMA((heads,)),
         ],
         compiler_params=pltpu.CompilerParams(
-            collective_id=0, has_side_effects=True, vmem_limit_bytes=63 << 20
+            collective_id=0, has_side_effects=True, vmem_limit_bytes=56 << 20
         ),
         cost_estimate=pl.CostEstimate(flops=2 << 30, bytes_accessed=8 << 20, transcendentals=0),
     )(*args)

time: 30.2 us -> 28.2 us (0.934)
  local copies, waits for them, and re-layouts: 2.31 us -> 0.97 us
  Pallas kernels: 27.7 us -> 27 us
    unnamed x1, local copies, waits for them, and re-layouts: 2.31 us -> 0.97 us
    pallas_call x1, Pallas kernels: 27.7 us -> 27 us  [shards(): pl.pallas_call(functools.partial(kernel, n), out_shape=pltpu.VMEM((rows,...]
where the time goes in v4:
time: 28.2 us; the launch traced here: 28 us
  Pallas kernels  27 us (96%)
  local copies, waits for them, and re-layouts  0.97 us (3%)
    pallas_call x1, Pallas kernels, shards(): pl.pallas_call(functools.partial(kernel, n), out_shape=pltpu.VMEM((rows,...  27 us
    unnamed x1, local copies, waits for them, and re-layouts  0.97 us

profile of v4, /device:TPU:26, one launch (start us, length us, event | category | flops | bytes accessed | tf_op | source)
XLA Modules:
  0.0 28.0 jit_solution(17353582727796468500)
XLA Ops:
  0.0 27.0 %shard_map.64 = f32[256,1024]{1,0:T(8,128)S(1)} custom-call(f32[256,1024]{1,0:T(8,128)} %q_hbm.1, f32[256,1024]{1,0:T(8,128)} %k_hbm.1, f32[256,1024]{1,0:T(8,128)} %v_hbm.1, f32[6,8,256]{2,1,0:T(8,128)} %bitcast.1, f32[8,8,256]{2,1,0:T(8,128)} %pw_hbm.1, f32[8,1024,128]{2,1,0:T(8,128)} %ps_hbm.1), custom_call_target="tpu_custom_call" | custom-call | flops 2147483648 | bytes 8388608 | tf_op jit(solution)/shard_map/pallas_call | solution.py:270
  27.0 1.0 %copy.8 = f32[256,1024]{1,0:T(8,128)} copy(f32[256,1024]{1,0:T(8,128)S(1)} %shard_map.64) | data formatting | bytes 2097152

commit v5 on v4

--- a/solution.py
+++ b/solution.py
@@ -79,8 +79,6 @@
     def _():
         pl.semaphore_signal(barrier, inc=1, device_id=device(jnp.maximum(me - 2, 0)))
 
-    pl.semaphore_wait(barrier, stages + onward.astype(jnp.int32) + upper.astype(jnp.int32))
-
     def stage_copy(b, h):
         return pltpu.make_async_remote_copy(
             src_ref=run.at[b, h], dst_ref=got.at[b, h],
@@ -138,15 +136,22 @@
     loads[0].wait()
     loads[1].wait()
 
-    def states(j, _):
-        h = leaving(j)
+    def own_state(h):
         kh = left(k[:, cols(h)], 0)
         vh = right(v[:, cols(h)], 0)
         run[0, h] = dot(kh, vh, ((0,), (0,)))
-        when(sends(0), stage_copy(0, h).start)
+
+    own_state(leaving(0))
+    pl.semaphore_wait(barrier, stages + onward.astype(jnp.int32) + upper.astype(jnp.int32))
+    when(sends(0), lambda: stage_copy(0, leaving(0)).start())
+
+    def states(j, _):
+        h = leaving(j)
+        own_state(h)
+        when(sends(0), lambda: stage_copy(0, h).start())
         return 0
 
-    lax.fori_loop(0, heads, states, 0)
+    lax.fori_loop(1, heads, states, 0)
 
     for load in loads[2:]:
         load.wait()
@@ -199,6 +204,9 @@
 
         when(receives(b), arrived)
 
+    def level(b, j):
+        h = arriving(j)
+
         @pl.when(bit(b))
         def _():
             add_level(h, got[b, h], buckets + 1 + b)
@@ -232,11 +240,15 @@
         def _():
             fn(h)
 
+    own(0)
+
     def step(i, _):
-        at(i, own)
         for b in range(stages):
             at(i - b, functools.partial(stage, b))
         at(i - stages, relay)
+        at(i + 1, own)
+        for b in range(stages):
+            at(i - b, functools.partial(level, b))
         at(i - stages - 2, finish)
         return 0
 

time: 28.2 us -> 28.7 us (1.018)
  Pallas kernels: 27 us -> 27.3 us
where the time goes in v5:
time: 28.7 us; the launch traced here: 28.3 us
  Pallas kernels  27.3 us (95%)
  local copies, waits for them, and re-layouts  0.97 us (3%)
    pallas_call x1, Pallas kernels, shards(): pl.pallas_call(functools.partial(kernel, n), out_shape=pltpu.VMEM((rows,...  27.3 us
    unnamed x1, local copies, waits for them, and re-layouts  0.97 us

profile of v5, /device:TPU:26, one launch (start us, length us, event | category | flops | bytes accessed | tf_op | source)
XLA Modules:
  0.0 28.3 jit_solution(17436824186615376081)
XLA Ops:
  0.0 27.3 %shard_map.64 = f32[256,1024]{1,0:T(8,128)S(1)} custom-call(f32[256,1024]{1,0:T(8,128)} %q_hbm.1, f32[256,1024]{1,0:T(8,128)} %k_hbm.1, f32[256,1024]{1,0:T(8,128)} %v_hbm.1, f32[6,8,256]{2,1,0:T(8,128)} %bitcast.1, f32[8,8,256]{2,1,0:T(8,128)} %pw_hbm.1, f32[8,1024,128]{2,1,0:T(8,128)} %ps_hbm.1), custom_call_target="tpu_custom_call" | custom-call | flops 2147483648 | bytes 8388608 | tf_op jit(solution)/shard_map/pallas_call | solution.py:282
  27.3 1.0 %copy.8 = f32[256,1024]{1,0:T(8,128)} copy(f32[256,1024]{1,0:T(8,128)S(1)} %shard_map.64) | data formatting | bytes 2097152

commit v6 on v5

--- a/solution.py
+++ b/solution.py
@@ -240,13 +240,11 @@
         def _():
             fn(h)
 
-    own(0)
-
     def step(i, _):
+        at(i, own)
         for b in range(stages):
             at(i - b, functools.partial(stage, b))
         at(i - stages, relay)
-        at(i + 1, own)
         for b in range(stages):
             at(i - b, functools.partial(level, b))
         at(i - stages - 2, finish)

time: 28.7 us -> 28.6 us (level)
  no operation moved by 1% of the time
where the time goes in v6:
time: 28.6 us; the launch traced here: 28.2 us
  Pallas kernels  27.3 us (95%)
  local copies, waits for them, and re-layouts  0.97 us (3%)
    pallas_call x1, Pallas kernels, shards(): pl.pallas_call(functools.partial(kernel, n), out_shape=pltpu.VMEM((rows,...  27.3 us
    unnamed x1, local copies, waits for them, and re-layouts  0.97 us

profile of v6, /device:TPU:26, one launch (start us, length us, event | category | flops | bytes accessed | tf_op | source)
XLA Modules:
  0.0 28.2 jit_solution(13293252775267253923)
XLA Ops:
  0.0 27.3 %shard_map.64 = f32[256,1024]{1,0:T(8,128)S(1)} custom-call(f32[256,1024]{1,0:T(8,128)} %q_hbm.1, f32[256,1024]{1,0:T(8,128)} %k_hbm.1, f32[256,1024]{1,0:T(8,128)} %v_hbm.1, f32[6,8,256]{2,1,0:T(8,128)} %bitcast.1, f32[8,8,256]{2,1,0:T(8,128)} %pw_hbm.1, f32[8,1024,128]{2,1,0:T(8,128)} %ps_hbm.1), custom_call_target="tpu_custom_call" | custom-call | flops 2147483648 | bytes 8388608 | tf_op jit(solution)/shard_map/pallas_call | solution.py:280
  27.3 1.0 %copy.8 = f32[256,1024]{1,0:T(8,128)} copy(f32[256,1024]{1,0:T(8,128)S(1)} %shard_map.64) | data formatting | bytes 2097152

commit v7 on v6

--- a/solution.py
+++ b/solution.py
@@ -64,7 +64,7 @@
             [(k_hbm, k), (v_hbm, v), (q_hbm, q), (lw_hbm, lw), (pw_hbm, pw), (ps_hbm, ps)]
         )
     ]
-    for load in loads:
+    for load in loads[:2]:
         load.start()
 
     barrier = pltpu.get_barrier_semaphore()
@@ -135,6 +135,8 @@
 
     loads[0].wait()
     loads[1].wait()
+    for load in loads[2:]:
+        load.start()
 
     def own_state(h):
         kh = left(k[:, cols(h)], 0)
@@ -244,9 +246,8 @@
         at(i, own)
         for b in range(stages):
             at(i - b, functools.partial(stage, b))
+            at(i - b, functools.partial(level, b))
         at(i - stages, relay)
-        for b in range(stages):
-            at(i - b, functools.partial(level, b))
         at(i - stages - 2, finish)
         return 0
 

time: 28.6 us -> 28.6 us (level)
  the two profiles are of different devices: /device:TPU:26 before, /device:TPU:28 now
where the time goes in v7:
time: 28.6 us; the launch traced here: 28.4 us
  Pallas kernels  27.4 us (96%)
  local copies, waits for them, and re-layouts  0.97 us (3%)
    pallas_call x1, Pallas kernels, shards(): pl.pallas_call(functools.partial(kernel, n), out_shape=pltpu.VMEM((rows,...  27.4 us
    unnamed x1, local copies, waits for them, and re-layouts  0.97 us

profile of v7, /device:TPU:28, one launch (start us, length us, event | category | flops | bytes accessed | tf_op | source)
XLA Modules:
  0.0 28.4 jit_solution(7026826125739158728)
XLA Ops:
  0.0 27.4 %shard_map.64 = f32[256,1024]{1,0:T(8,128)S(1)} custom-call(f32[256,1024]{1,0:T(8,128)} %q_hbm.1, f32[256,1024]{1,0:T(8,128)} %k_hbm.1, f32[256,1024]{1,0:T(8,128)} %v_hbm.1, f32[6,8,256]{2,1,0:T(8,128)} %bitcast.1, f32[8,8,256]{2,1,0:T(8,128)} %pw_hbm.1, f32[8,1024,128]{2,1,0:T(8,128)} %ps_hbm.1), custom_call_target="tpu_custom_call" | custom-call | flops 2147483648 | bytes 8388608 | tf_op jit(solution)/shard_map/pallas_call | solution.py:281
  27.5 1.0 %copy.8 = f32[256,1024]{1,0:T(8,128)} copy(f32[256,1024]{1,0:T(8,128)S(1)} %shard_map.64) | data formatting | bytes 2097152
